TPU v7x, 512 devices: a whole 4x8x8 slice. The times are simulated.
512 devices in a mesh: region: 16 (over y, core), tile: 32 (over x, z).
Axes of the slice: x: 4, y: 8, z: 8, core: 2. Of those that a mesh axis runs over, the one named last changes fastest.
Arguments:
- prior_pressure: float32 [64, 4, 64, 4096], P(None, None, 'region', 'tile'), may hold values from -6 to 6
- infiltration_source: float32 [64, 64, 4096], P(None, 'region', 'tile'), may hold values from -6 to 6
- soil_class: int32 [4, 64, 4096], P(None, 'region', 'tile'), may hold values from 0 to 11
- soil_k: float32 [12], replicated, may hold values from 0.02 to 0.2
- obs_index: int32 [131072], P(('region', 'tile')), may hold values from 0 to 2047
- obs_value: float32 [131072], P(('region', 'tile')), may hold values from -6 to 6
- obs_var: float32 [131072], P(('region', 'tile')), may hold values from 0.5 to 8
- obs_count: int32 [512], P(('region', 'tile')), may hold values from 1 to 256, as said below
Outputs:
- analysis: float32 [64, 4, 64, 4096], P(None, None, 'region', 'tile')
Inputs may be any that keep to these rules, and one draw needn't show every extreme that they name: `obs_count`: at least one block has all 256 slots live.
All inputs are finite; a program needn't handle non-finite values.
Results may differ from a plain program's by a relative error of at most 0.00019.
Values sent between devices are 32-bit elements; how exact they have to be, the bound alone decides.
No kernel may reach another device: no remote copies, remote signals or barrier semaphores. Data moves between devices by JAX's collectives and lax.ppermute only.
A program may use at most 64 MiB of HBM per device.

v0:
```python
import jax
import jax.numpy as jnp
from jax import lax
from jax.sharding import PartitionSpec as P

STEPS = 3
step_dt = 0.25
vert_share = 0.5


def extended(block, sides, width):
    for axis, dim in sides:
        count = lax.axis_size(axis)
        forward = [(i, i + 1) for i in range(count - 1)]
        backward = [(target, source) for source, target in forward]
        low = lax.ppermute(
            lax.slice_in_dim(block, block.shape[dim] - width, None, axis=dim), axis, forward
        )
        high = lax.ppermute(lax.slice_in_dim(block, 0, width, axis=dim), axis, backward)
        block = jnp.concatenate([low, block, high], axis=dim)
    return block


def lookup(soil_class, soil_k):
    total = jnp.zeros(soil_class.shape, jnp.float32)
    for index in range(soil_k.shape[0]):
        total = total + jnp.where(soil_class == index, soil_k[index], 0.0)
    return total


def cholesky_lower(matrix):
    order = matrix.shape[0]
    places = jnp.arange(order, dtype=jnp.int32)

    def column_step(column, lower):
        onehot = (places == column.astype(jnp.int32)).astype(matrix.dtype)
        row_now = jnp.dot(onehot, lower, precision=lax.Precision.HIGHEST)
        remain = jnp.dot(matrix, onehot, precision=lax.Precision.HIGHEST) - jnp.dot(
            lower, row_now, precision=lax.Precision.HIGHEST
        )
        pivot = jnp.sqrt(jnp.sum(remain * onehot))
        fresh = jnp.where(
            places >= column.astype(jnp.int32), remain / pivot, jnp.zeros_like(remain)
        )
        return lower + fresh[:, None] * onehot[None, :]

    return lax.fori_loop(0, order, column_step, jnp.zeros_like(matrix))


def lower_inverse(lower):
    order = lower.shape[0]
    places = jnp.arange(order, dtype=jnp.int32)

    def row_step(row, solved):
        onehot = (places == row.astype(jnp.int32)).astype(lower.dtype)
        row_now = jnp.dot(onehot, lower, precision=lax.Precision.HIGHEST)
        pivot = jnp.sum(row_now * onehot)
        fresh = (onehot - jnp.dot(row_now, solved, precision=lax.Precision.HIGHEST)) / pivot
        return solved + onehot[:, None] * fresh[None, :]

    return lax.fori_loop(0, order, row_step, jnp.zeros_like(lower))


def update(padded, bordered_permeability, push):
    cond = bordered_permeability[None] * (0.5 + jax.nn.sigmoid(padded))
    center = padded[:, :, 1:-1, 1:-1]
    kcen = cond[:, :, 1:-1, 1:-1]
    flux = jnp.zeros_like(center)
    for rows, cols in (
        (slice(2, None), slice(1, -1)),
        (slice(None, -2), slice(1, -1)),
        (slice(1, -1), slice(2, None)),
        (slice(1, -1), slice(None, -2)),
    ):
        flux = flux + 0.5 * (kcen + cond[:, :, rows, cols]) * (padded[:, :, rows, cols] - center)
    upward = vert_share * 0.5 * (kcen[:, 1:] + kcen[:, :-1]) * (center[:, 1:] - center[:, :-1])
    flux = (
        flux
        + jnp.pad(upward, ((0, 0), (0, 1), (0, 0), (0, 0)))
        - jnp.pad(upward, ((0, 0), (1, 0), (0, 0), (0, 0)))
    )
    flux = flux + jnp.pad(push[:, None], ((0, 0), (0, center.shape[1] - 1), (0, 0), (0, 0)))
    return center + step_dt * flux


def propagate_pressure(state, bordered_permeability, infiltration_source):
    padded = extended(state, (("region", 2), ("tile", 3)), 1)
    return update(padded, bordered_permeability, infiltration_source)


def shards(
    prior_pressure,
    infiltration_source,
    soil_class,
    soil_k,
    obs_index,
    obs_value,
    obs_var,
    obs_count,
):
    realization_vectors = prior_pressure.shape[0]
    depth = 1
    bordered_permeability = extended(
        lookup(soil_class, soil_k), (("region", 1), ("tile", 2)), depth
    )
    predicted_pressure = prior_pressure
    for step in range(STEPS):
        predicted_pressure = propagate_pressure(
            predicted_pressure, bordered_permeability, infiltration_source
        )
    unrolled_vector = predicted_pressure.reshape(realization_vectors, -1)
    measured_pressure = jnp.take(unrolled_vector, obs_index, axis=1)
    live = (jnp.arange(obs_index.shape[0], dtype=jnp.int32) < obs_count[0]).astype(jnp.float32)
    weight = live / jnp.sqrt(obs_var)
    hmean = jnp.mean(measured_pressure, axis=0)
    anomal = (measured_pressure - hmean) * weight
    innov = (obs_value - hmean) * weight
    gram = jnp.dot(anomal, anomal.T, precision=lax.Precision.HIGHEST)
    bvec = jnp.dot(anomal, innov, precision=lax.Precision.HIGHEST)
    eye = jnp.eye(realization_vectors, dtype=jnp.float32)
    gram, bvec = lax.psum((gram, bvec), ("region", "tile"))
    lower = cholesky_lower((realization_vectors - 1.0) * eye + gram)
    inverse = lower_inverse(lower)
    wmean = jnp.dot(
        inverse.T,
        jnp.dot(inverse, bvec, precision=lax.Precision.HIGHEST),
        precision=lax.Precision.HIGHEST,
    )
    wroot = inverse.T * jnp.sqrt(realization_vectors - 1.0)
    blending_factor = wroot + wmean[:, None]
    sample_average = jnp.mean(predicted_pressure, axis=0)
    deviation_matrix = (predicted_pressure - sample_average).reshape(realization_vectors, -1)
    propagated_vector = jnp.dot(
        blending_factor.T, deviation_matrix, precision=lax.Precision.HIGHEST
    ).reshape(predicted_pressure.shape)
    return sample_average + propagated_vector


def solution(mesh):
    return jax.shard_map(
        shards,
        mesh=mesh,
        in_specs=(
            P(None, None, "region", "tile"),
            P(None, "region", "tile"),
            P(None, "region", "tile"),
            P(),
            P(("region", "tile")),
            P(("region", "tile")),
            P(("region", "tile")),
            P(("region", "tile")),
        ),
        out_specs=P(None, None, "region", "tile"),
        check_vma=False,
    )
```

profile of v0, /device:TPU:1, one launch (start us, length us, event | category | flops | bytes accessed | tf_op | source)
XLA Modules:
  0.0 435.6 jit_solution(1766568834195470314)
XLA Ops:
  0.0 1.8 fusion.141
  1.8 8.3 %select_add_fusion.1 = f32[4,4,128]{2,1,0:T(4,128)S(1)} fusion(s32[4,4,128]{2,1,0:T(4,128)} %param.14, f32[]{:T(128)} %bitcast.11, f32[]{:T(128)} %bitcast.10, f32[]{:T(128)} %bitcast.9, f32[]{:T(128)} %bitcast.8, f32[]{:T(128)} %bitcast.7, f32[]{:T(128)} %bitcast.6, f32[]{:T(128)} %bitcast.5, f32[]{:T(128)} %bitcast.4, f32[]{:T(128)} %bitcast.3, ...), kind=kLoop, calls=%fused_computation.194 | loop fusion | flops 71680 | bytes 16432 | tf_op jit(solution)/shard_map/add | solution.py:27
  10.1 4.6 %collective-permute-start = (f32[4,1,128]{2,1,0:T(1,128)S(1)}, f32[4,1,128]{2,1,0:T(1,128)S(1)}, u32[]{:S(2)}, u32[]{:S(2)}) collective-permute-start(f32[4,1,128]{2,1,0:T(1,128)S(1)} %get-tuple-element.244), channel_id=1, source_target_pairs={{0,32},{32,64},{64,96},{96,128},{128,160},{160,192},{192,224},{224... | collective-permute-start | bytes 6152 | tf_op jit(solution)/shard_map/ppermute | solution.py:16
  14.7 5.5 %collective-permute-start.1 = (f32[4,1,128]{2,1,0:T(1,128)S(1)}, f32[4,1,128]{2,1,0:T(1,128)S(1)}, u32[]{:S(2)}, u32[]{:S(2)}) collective-permute-start(f32[4,1,128]{2,1,0:T(1,128)S(1)} %get-tuple-element.245), channel_id=1, source_target_pairs={{32,0},{64,32},{96,64},{128,96},{160,128},{192,160},{224,192},{256... | collective-permute-start | bytes 6152 | tf_op jit(solution)/shard_map/ppermute | solution.py:19
  21.4 1.9 collective-permute-start.4
  23.3 2.4 collective-permute-start.5
  26.5 2.3 collective-permute-start.2
  32.0 4.1 collective-permute-start.6
  38.8 2.6 collective-permute-done.7
  44.5 5.1 %collective-permute-start.8 = (f32[64,4,1,128]{3,0,2,1:T(8,128)S(1)}, f32[64,4,1,128]{3,0,2,1:T(8,128)S(1)}, u32[]{:S(2)}, u32[]{:S(2)}) collective-permute-start(f32[64,4,1,128]{3,0,2,1:T(8,128)S(1)} %get-tuple-element.238), channel_id=1, source_target_pairs={{0,32},{32,64},{64,96},{96,128},{128,160},{160,192},{192,224},{224... | collective-permute-start | bytes 393224 | tf_op jit(solution)/shard_map/ppermute | solution.py:16
  49.6 1.9 collective-permute-start.9
  51.5 4.3 collective-permute-done.9
  56.6 5.2 %collective-permute-start.10 = (f32[64,4,6,1]{0,1,3,2:T(4,128)S(1)}, f32[64,4,6,1]{0,1,3,2:T(4,128)S(1)}, u32[]{:S(2)}, u32[]{:S(2)}) collective-permute-start(f32[64,4,6,1]{0,1,3,2:T(4,128)S(1)} %copy.60), channel_id=1, source_target_pairs={{0,1},{1,2},{2,3},{3,4},{4,5},{5,6},{6,7},{7,8},{8,9},{9,10},{10,1... | collective-permute-start | bytes 18440 | tf_op jit(solution)/shard_map/ppermute | solution.py:16
  62.1 1.3 collective-permute-start.11
  63.7 4.3 collective-permute-done.11
  70.4 2.9 collective-permute-start.12
  73.4 1.9 collective-permute-start.13
  75.3 4.3 collective-permute-done.13
  80.3 4.9 %collective-permute-start.14 = (f32[64,4,6,1]{0,1,3,2:T(4,128)S(1)}, f32[64,4,6,1]{0,1,3,2:T(4,128)S(1)}, u32[]{:S(2)}, u32[]{:S(2)}) collective-permute-start(f32[64,4,6,1]{0,1,3,2:T(4,128)S(1)} %copy.66), channel_id=1, source_target_pairs={{0,1},{1,2},{2,3},{3,4},{4,5},{5,6},{6,7},{7,8},{8,9},{9,10},{10,1... | collective-permute-start | bytes 18440 | tf_op jit(solution)/shard_map/ppermute | solution.py:16
  85.5 1.3 collective-permute-start.15
  87.8 2.4 collective-permute-done.15
  94.9 106.0 %all-reduce.7 = (f32[64,64]{1,0:T(8,128)S(1)}, f32[64]{0:T(128)S(1)}) all-reduce(f32[64,64]{1,0:T(8,128)S(1)} %fusion.112, f32[64]{0:T(128)S(1)} %convolution_bitcast_fusion.6), channel_id=1, replica_groups=mesh['region'=16,'tile'=32] {'region','tile'}, use_global_device_ids=true, to_apply=%region_2.3 | all-reduce | flops 4160 | bytes 33280 | tf_op jit(solution)/shard_map/psum | solution.py:121
  200.9 120.4 %while.30 = (s32[]{:T(128)}, f32[64,64]{1,0:T(8,128)S(1)}, f32[64,64]{1,0:T(8,128)S(1)}, s32[]{:T(128)}, s32[]{:T(128)}) while((s32[]{:T(128)}, f32[64,64]{1,0:T(8,128)S(1)}, f32[64,64]{1,0:T(8,128)S(1)}, s32[]{:T(128)}, s32[]{:T(128)}) %tuple.90), condition=%wide.region_5.6_spmd.clone.clone, body=%wide.region_3.5_spmd.clone.clone.sunk | while | flops 168642 | bytes 84589 | solution.py:47
  321.2 111.2 %while.29 = (s32[]{:T(128)}, f32[64,64]{1,0:T(8,128)S(1)}, f32[64,64]{1,0:T(8,128)S(1)}, s32[]{:T(128)}, s32[]{:T(128)}) while((s32[]{:T(128)}, f32[64,64]{1,0:T(8,128)S(1)}, f32[64,64]{1,0:T(8,128)S(1)}, s32[]{:T(128)}, s32[]{:T(128)}) %tuple.93), condition=%wide.region_8.9_spmd.clone, body=%wide.region_6.8_spmd.clone.sunk | while | flops 115330 | bytes 67164 | solution.py:61
  (734 shorter events, 210.1 us)
Async XLA Ops:
  0.0 30.1 %copy-start = (f32[64,4,4,128]{3,2,1,0:T(4,128)S(1)}, f32[64,4,4,128]{3,2,1,0:T(4,128)}, u32[]{:S(2)}) copy-start(f32[64,4,4,128]{3,2,1,0:T(4,128)} %param.12) | copy-start | bytes 1572868
  0.0 25.8 %copy-start.7 = (f32[64,4,128]{2,1,0:T(4,128)S(1)}, f32[64,4,128]{2,1,0:T(4,128)}, u32[]{:S(2)}) copy-start(f32[64,4,128]{2,1,0:T(4,128)} %param.13) | copy-start | bytes 393220
  10.1 15.7 %collective-permute-start = (f32[4,1,128]{2,1,0:T(1,128)S(1)}, f32[4,1,128]{2,1,0:T(1,128)S(1)}, u32[]{:S(2)}, u32[]{:S(2)}) collective-permute-start(f32[4,1,128]{2,1,0:T(1,128)S(1)} %get-tuple-element.244), channel_id=1, source_target_pairs={{0,32},{32,64},{64,96},{96,128},{128,160},{160,192},{192,224},{224... | collective-permute-start | bytes 6152 | tf_op jit(solution)/shard_map/ppermute | solution.py:16
  14.7 11.1 %collective-permute-start.1 = (f32[4,1,128]{2,1,0:T(1,128)S(1)}, f32[4,1,128]{2,1,0:T(1,128)S(1)}, u32[]{:S(2)}, u32[]{:S(2)}) collective-permute-start(f32[4,1,128]{2,1,0:T(1,128)S(1)} %get-tuple-element.245), channel_id=1, source_target_pairs={{32,0},{64,32},{96,64},{128,96},{160,128},{192,160},{224,192},{256... | collective-permute-start | bytes 6152 | tf_op jit(solution)/shard_map/ppermute | solution.py:19
  21.4 8.6 %collective-permute-start.4 = (f32[64,4,1,128]{3,0,2,1:T(8,128)S(1)}, f32[64,4,1,128]{3,0,2,1:T(8,128)S(1)}, u32[]{:S(2)}, u32[]{:S(2)}) collective-permute-start(f32[64,4,1,128]{3,0,2,1:T(8,128)S(1)} %get-tuple-element.241), channel_id=1, source_target_pairs={{0,32},{32,64},{64,96},{96,128},{128,160},{160,192},{192,224},{224... | collective-permute-start | bytes 393224 | tf_op jit(solution)/shard_map/ppermute | solution.py:16
  23.3 6.9 %collective-permute-start.5 = (f32[64,4,1,128]{3,0,2,1:T(8,128)S(1)}, f32[64,4,1,128]{3,0,2,1:T(8,128)S(1)}, u32[]{:S(2)}, u32[]{:S(2)}) collective-permute-start(f32[64,4,1,128]{3,0,2,1:T(8,128)S(1)} %get-tuple-element.240), channel_id=1, source_target_pairs={{32,0},{64,32},{96,64},{128,96},{160,128},{192,160},{224,192},{256... | collective-permute-start | bytes 393224 | tf_op jit(solution)/shard_map/ppermute | solution.py:19
  26.5 11.1 %collective-permute-start.2 = (f32[4,6,1]{2,1,0:T(8,128)}, f32[4,6,1]{2,1,0:T(8,128)}, u32[]{:S(2)}, u32[]{:S(2)}) collective-permute-start(f32[4,6,1]{2,1,0:T(8,128)} %get-tuple-element.242), channel_id=1, source_target_pairs={{0,1},{1,2},{2,3},{3,4},{4,5},{5,6},{6,7},{7,8},{8,9},{9,10},{10,1... | collective-permute-start | bytes 296 | tf_op jit(solution)/shard_map/ppermute | solution.py:16
  28.8 8.9 %collective-permute-start.3 = (f32[4,6,1]{2,1,0:T(8,128)}, f32[4,6,1]{2,1,0:T(8,128)}, u32[]{:S(2)}, u32[]{:S(2)}) collective-permute-start(f32[4,6,1]{2,1,0:T(8,128)} %get-tuple-element.243), channel_id=1, source_target_pairs={{1,0},{2,1},{3,2},{4,3},{5,4},{6,5},{7,6},{8,7},{9,8},{10,9},{11,1... | collective-permute-start | bytes 296 | tf_op jit(solution)/shard_map/ppermute | solution.py:19
  32.0 6.5 %collective-permute-start.6 = (f32[64,4,6,1]{0,1,3,2:T(4,128)S(1)}, f32[64,4,6,1]{0,1,3,2:T(4,128)S(1)}, u32[]{:S(2)}, u32[]{:S(2)}) collective-permute-start(f32[64,4,6,1]{0,1,3,2:T(4,128)S(1)} %copy.44), channel_id=1, source_target_pairs={{0,1},{1,2},{2,3},{3,4},{4,5},{5,6},{6,7},{7,8},{8,9},{9,10},{10,1... | collective-permute-start | bytes 18440 | tf_op jit(solution)/shard_map/ppermute | solution.py:16
  36.3 5.1 %collective-permute-start.7 = (f32[64,4,6,1]{0,1,3,2:T(4,128)S(1)}, f32[64,4,6,1]{0,1,3,2:T(4,128)S(1)}, u32[]{:S(2)}, u32[]{:S(2)}) collective-permute-start(f32[64,4,6,1]{0,1,3,2:T(4,128)S(1)} %copy.45), channel_id=1, source_target_pairs={{1,0},{2,1},{3,2},{4,3},{5,4},{6,5},{7,6},{8,7},{9,8},{10,9},{11,1... | collective-permute-start | bytes 18440 | tf_op jit(solution)/shard_map/ppermute | solution.py:19
  38.5 4.0 copy-start.1
  42.5 1.0 copy-start.6
  44.5 7.0 %collective-permute-start.8 = (f32[64,4,1,128]{3,0,2,1:T(8,128)S(1)}, f32[64,4,1,128]{3,0,2,1:T(8,128)S(1)}, u32[]{:S(2)}, u32[]{:S(2)}) collective-permute-start(f32[64,4,1,128]{3,0,2,1:T(8,128)S(1)} %get-tuple-element.238), channel_id=1, source_target_pairs={{0,32},{32,64},{64,96},{96,128},{128,160},{160,192},{192,224},{224... | collective-permute-start | bytes 393224 | tf_op jit(solution)/shard_map/ppermute | solution.py:16
  49.6 6.3 %collective-permute-start.9 = (f32[64,4,1,128]{3,0,2,1:T(8,128)S(1)}, f32[64,4,1,128]{3,0,2,1:T(8,128)S(1)}, u32[]{:S(2)}, u32[]{:S(2)}) collective-permute-start(f32[64,4,1,128]{3,0,2,1:T(8,128)S(1)} %get-tuple-element.239), channel_id=1, source_target_pairs={{32,0},{64,32},{96,64},{128,96},{160,128},{192,160},{224,192},{256... | collective-permute-start | bytes 393224 | tf_op jit(solution)/shard_map/ppermute | solution.py:19
  56.3 7.1 %copy-start.8 = (s32[256]{0:T(256)S(1)}, s32[256]{0:T(256)}, u32[]{:S(2)}) copy-start(s32[256]{0:T(256)} %param.16) | copy-start | bytes 3076
  56.3 12.1 %copy-start.2 = (f32[4,6,130]{2,1,0:T(8,128)S(1)}, f32[4,6,130]{2,1,0:T(8,128)}, u32[]{:S(2)}) copy-start(f32[4,6,130]{2,1,0:T(8,128)} %copy-done.1) | copy-start | bytes 37444
  56.6 6.8 %collective-permute-start.10 = (f32[64,4,6,1]{0,1,3,2:T(4,128)S(1)}, f32[64,4,6,1]{0,1,3,2:T(4,128)S(1)}, u32[]{:S(2)}, u32[]{:S(2)}) collective-permute-start(f32[64,4,6,1]{0,1,3,2:T(4,128)S(1)} %copy.60), channel_id=1, source_target_pairs={{0,1},{1,2},{2,3},{3,4},{4,5},{5,6},{6,7},{7,8},{8,9},{9,10},{10,1... | collective-permute-start | bytes 18440 | tf_op jit(solution)/shard_map/ppermute | solution.py:16
  62.1 5.9 %collective-permute-start.11 = (f32[64,4,6,1]{0,1,3,2:T(4,128)S(1)}, f32[64,4,6,1]{0,1,3,2:T(4,128)S(1)}, u32[]{:S(2)}, u32[]{:S(2)}) collective-permute-start(f32[64,4,6,1]{0,1,3,2:T(4,128)S(1)} %copy.61), channel_id=1, source_target_pairs={{1,0},{2,1},{3,2},{4,3},{5,4},{6,5},{7,6},{8,7},{9,8},{10,9},{11,1... | collective-permute-start | bytes 18440 | tf_op jit(solution)/shard_map/ppermute | solution.py:19
  70.4 4.9 %collective-permute-start.12 = (f32[64,4,1,128]{3,0,2,1:T(8,128)S(1)}, f32[64,4,1,128]{3,0,2,1:T(8,128)S(1)}, u32[]{:S(2)}, u32[]{:S(2)}) collective-permute-start(f32[64,4,1,128]{3,0,2,1:T(8,128)S(1)} %get-tuple-element.236), channel_id=1, source_target_pairs={{0,32},{32,64},{64,96},{96,128},{128,160},{160,192},{192,224},{224... | collective-permute-start | bytes 393224 | tf_op jit(solution)/shard_map/ppermute | solution.py:16
  73.4 6.3 %collective-permute-start.13 = (f32[64,4,1,128]{3,0,2,1:T(8,128)S(1)}, f32[64,4,1,128]{3,0,2,1:T(8,128)S(1)}, u32[]{:S(2)}, u32[]{:S(2)}) collective-permute-start(f32[64,4,1,128]{3,0,2,1:T(8,128)S(1)} %get-tuple-element.237), channel_id=1, source_target_pairs={{32,0},{64,32},{96,64},{128,96},{160,128},{192,160},{224,192},{256... | collective-permute-start | bytes 393224 | tf_op jit(solution)/shard_map/ppermute | solution.py:19
  80.3 7.1 %collective-permute-start.14 = (f32[64,4,6,1]{0,1,3,2:T(4,128)S(1)}, f32[64,4,6,1]{0,1,3,2:T(4,128)S(1)}, u32[]{:S(2)}, u32[]{:S(2)}) collective-permute-start(f32[64,4,6,1]{0,1,3,2:T(4,128)S(1)} %copy.66), channel_id=1, source_target_pairs={{0,1},{1,2},{2,3},{3,4},{4,5},{5,6},{6,7},{7,8},{8,9},{9,10},{10,1... | collective-permute-start | bytes 18440 | tf_op jit(solution)/shard_map/ppermute | solution.py:16
  85.5 4.7 %collective-permute-start.15 = (f32[64,4,6,1]{0,1,3,2:T(4,128)S(1)}, f32[64,4,6,1]{0,1,3,2:T(4,128)S(1)}, u32[]{:S(2)}, u32[]{:S(2)}) collective-permute-start(f32[64,4,6,1]{0,1,3,2:T(4,128)S(1)} %copy.67), channel_id=1, source_target_pairs={{1,0},{2,1},{3,2},{4,3},{5,4},{6,5},{7,6},{8,7},{9,8},{10,9},{11,1... | collective-permute-start | bytes 18440 | tf_op jit(solution)/shard_map/ppermute | solution.py:19
  92.6 1.3 copy-start.9
  92.6 1.3 copy-start.10
  (3 other events, 2.2 us)
where the time goes:
time: 441 us; the launch traced here: 436 us
  matrix products  178 us (40%)
  blocking collectives  106 us (24%)
  starting transfers between devices  47.8 us (11%)
  loops' own time  45.1 us (10%)
  other arithmetic  26.4 us (6%)
  waiting for transfers between devices  18 us (4%)
  local copies, waits for them, and re-layouts  13.4 us (3%)
    psum x1, blocking collectives, shards(): gram, bvec = lax.psum((gram, bvec), ('region', 'tile'))  106 us
    dot_general x64, matrix products, column_step(): jnp.dot(lower, row_now, precision=lax.Precision.HIGHEST)  53.6 us
    dot_general x64, matrix products, row_step(): row_now = jnp.dot(onehot, lower, precision=lax.Precision.HIGHEST)  52.8 us
    dot_general x64, matrix products, row_step(): jnp.dot(row_now, solved, precision=lax.Precision.HIGHEST)  52.7 us
    another operation x1, loops' own time, cholesky_lower(): return lax.fori_loop(0, order, column_step, jnp.zeros_like(matrix))  44.6 us
    ppermute x8, starting transfers between devices, extended(): lax.ppermute(lax.slice_in_dim(block, block.shape[dim] - width, None, axis...  30.9 us
    ppermute x8, waiting for transfers between devices, extended(): lax.ppermute(lax.slice_in_dim(block, 0, width, axis=dim), axis, backward)  17.9 us
    ppermute x8, starting transfers between devices, extended(): lax.ppermute(lax.slice_in_dim(block, 0, width, axis=dim), axis, backward)  16.9 us
  transfers between devices with their start and end apart: 16, of which 5 were waited for; matrix products, arithmetic and copies ran while one was open for 1% of the time, Pallas kernels for 0%

commit v1 on v0

--- a/solution.py
+++ b/solution.py
@@ -118,7 +118,7 @@
     gram = jnp.dot(anomal, anomal.T, precision=lax.Precision.HIGHEST)
     bvec = jnp.dot(anomal, innov, precision=lax.Precision.HIGHEST)
     eye = jnp.eye(realization_vectors, dtype=jnp.float32)
-    gram, bvec = lax.psum((gram, bvec), ("region", "tile"))
+    gram, bvec = lax.psum(lax.psum((gram, bvec), "region"), "tile")
     lower = cholesky_lower((realization_vectors - 1.0) * eye + gram)
     inverse = lower_inverse(lower)
     wmean = jnp.dot(

time: 441 us -> 515 us (1.17)
  the two profiles are of different devices: /device:TPU:1 before, /device:TPU:32 now
where the time goes in v1:
time: 515 us; the launch traced here: 513 us
  blocking collectives  187 us (36%)
  matrix products  168 us (33%)
  starting transfers between devices  52.3 us (10%)
  loops' own time  47.6 us (9%)
  other arithmetic  26.4 us (5%)
  waiting for transfers between devices  16.7 us (3%)
  local copies, waits for them, and re-layouts  13.4 us (3%)
    psum x2, blocking collectives, shards(): gram, bvec = lax.psum(lax.psum((gram, bvec), 'region'), 'tile')  187 us
    dot_general x64, matrix products, column_step(): jnp.dot(lower, row_now, precision=lax.Precision.HIGHEST)  56.3 us
    dot_general x64, matrix products, row_step(): row_now = jnp.dot(onehot, lower, precision=lax.Precision.HIGHEST)  47.9 us
    another operation x1, loops' own time, cholesky_lower(): return lax.fori_loop(0, order, column_step, jnp.zeros_like(matrix))  47.2 us
    dot_general x64, matrix products, row_step(): jnp.dot(row_now, solved, precision=lax.Precision.HIGHEST)  45.2 us
    ppermute x8, starting transfers between devices, extended(): lax.ppermute(lax.slice_in_dim(block, block.shape[dim] - width, None, axis...  27.7 us
    ppermute x8, starting transfers between devices, extended(): lax.ppermute(lax.slice_in_dim(block, 0, width, axis=dim), axis, backward)  24.6 us
    ppermute x8, waiting for transfers between devices, extended(): lax.ppermute(lax.slice_in_dim(block, 0, width, axis=dim), axis, backward)  15.2 us
  transfers between devices with their start and end apart: 16, of which 7 were waited for; matrix products, arithmetic and copies ran while one was open for 1% of the time, Pallas kernels for 0%

profile of v1, /device:TPU:32, one launch (start us, length us, event | category | flops | bytes accessed | tf_op | source)
XLA Modules:
  0.0 512.6 jit_solution(3313087581010857931)
XLA Ops:
  0.0 1.8 fusion.141
  1.8 8.3 %select_add_fusion.1 = f32[4,4,128]{2,1,0:T(4,128)S(1)} fusion(s32[4,4,128]{2,1,0:T(4,128)} %param.14, f32[]{:T(128)} %bitcast.11, f32[]{:T(128)} %bitcast.10, f32[]{:T(128)} %bitcast.9, f32[]{:T(128)} %bitcast.8, f32[]{:T(128)} %bitcast.7, f32[]{:T(128)} %bitcast.6, f32[]{:T(128)} %bitcast.5, f32[]{:T(128)} %bitcast.4, f32[]{:T(128)} %bitcast.3, ...), kind=kLoop, calls=%fused_computation.194 | loop fusion | flops 71680 | bytes 16432 | tf_op jit(solution)/shard_map/add | solution.py:27
  10.1 1.9 collective-permute-start
  12.0 4.9 collective-permute-start.1
  18.1 1.9 collective-permute-start.4
  20.0 4.9 collective-permute-start.5
  25.6 4.9 collective-permute-start.2
  33.7 4.6 collective-permute-start.6
  38.6 1.3 collective-permute-start.7
  41.1 3.2 collective-permute-done.7
  47.4 1.9 collective-permute-start.8
  49.3 4.9 collective-permute-start.9
  54.9 1.8 collective-permute-done.9
  57.4 5.5 %collective-permute-start.10 = (f32[64,4,6,1]{0,1,3,2:T(4,128)S(1)}, f32[64,4,6,1]{0,1,3,2:T(4,128)S(1)}, u32[]{:S(2)}, u32[]{:S(2)}) collective-permute-start(f32[64,4,6,1]{0,1,3,2:T(4,128)S(1)} %copy.60), channel_id=1, source_target_pairs={{0,1},{1,2},{2,3},{3,4},{4,5},{5,6},{6,7},{7,8},{8,9},{9,10},{10,1... | collective-permute-start | bytes 18440 | tf_op jit(solution)/shard_map/ppermute | solution.py:16
  64.8 5.1 %collective-permute-done.11 = f32[64,4,6,1]{0,1,3,2:T(4,128)S(1)} collective-permute-done((f32[64,4,6,1]{0,1,3,2:T(4,128)S(1)}, f32[64,4,6,1]{0,1,3,2:T(4,128)S(1)}, u32[]{:S(2)}, u32[]{:S(2)}) %collective-permute-start.11) | collective-permute-done | bytes 6176 | tf_op jit(solution)/shard_map/ppermute | solution.py:19
  72.4 1.9 collective-permute-start.12
  74.3 4.9 collective-permute-start.13
  79.9 1.8 collective-permute-done.13
  82.4 5.1 %collective-permute-start.14 = (f32[64,4,6,1]{0,1,3,2:T(4,128)S(1)}, f32[64,4,6,1]{0,1,3,2:T(4,128)S(1)}, u32[]{:S(2)}, u32[]{:S(2)}) collective-permute-start(f32[64,4,6,1]{0,1,3,2:T(4,128)S(1)} %copy.66), channel_id=1, source_target_pairs={{0,1},{1,2},{2,3},{3,4},{4,5},{5,6},{6,7},{7,8},{8,9},{9,10},{10,1... | collective-permute-start | bytes 18440 | tf_op jit(solution)/shard_map/ppermute | solution.py:16
  90.1 3.3 collective-permute-done.15
  98.0 47.6 %all-reduce.8 = (f32[64,64]{1,0:T(8,128)S(1)}, f32[64]{0:T(128)S(1)}) all-reduce(f32[64,64]{1,0:T(8,128)S(1)} %fusion.112, f32[64]{0:T(128)S(1)} %convolution_bitcast_fusion.6), channel_id=1, replica_groups=mesh['region'=16,'tile'=32] {'region'}, use_global_device_ids=true, to_apply=%region_2.3 | all-reduce | flops 4160 | bytes 33280 | tf_op jit(solution)/shard_map/psum | solution.py:121
  145.6 139.4 %all-reduce.7 = (f32[64,64]{1,0:T(8,128)S(1)}, f32[64]{0:T(128)S(1)}) all-reduce(f32[64,64]{1,0:T(8,128)S(1)} %get-tuple-element.222, f32[64]{0:T(128)S(1)} %get-tuple-element.223), channel_id=1, replica_groups=mesh['region'=16,'tile'=32] {'tile'}, use_global_device_ids=true, to_apply=%region_3.4 | all-reduce | flops 4160 | bytes 33280 | tf_op jit(solution)/shard_map/psum | solution.py:121
  285.0 125.6 %while.30 = (s32[]{:T(128)}, f32[64,64]{1,0:T(8,128)S(1)}, f32[64,64]{1,0:T(8,128)S(1)}, s32[]{:T(128)}, s32[]{:T(128)}) while((s32[]{:T(128)}, f32[64,64]{1,0:T(8,128)S(1)}, f32[64,64]{1,0:T(8,128)S(1)}, s32[]{:T(128)}, s32[]{:T(128)}) %tuple.90), condition=%wide.region_6.7_spmd.clone.clone, body=%wide.region_4.6_spmd.clone.clone.sunk | while | flops 168642 | bytes 84589 | solution.py:47
  410.6 98.8 %while.29 = (s32[]{:T(128)}, f32[64,64]{1,0:T(8,128)S(1)}, f32[64,64]{1,0:T(8,128)S(1)}, s32[]{:T(128)}, s32[]{:T(128)}) while((s32[]{:T(128)}, f32[64,64]{1,0:T(8,128)S(1)}, f32[64,64]{1,0:T(8,128)S(1)}, s32[]{:T(128)}, s32[]{:T(128)}) %tuple.93), condition=%wide.region_9.10_spmd.clone, body=%wide.region_7.9_spmd.clone.sunk | while | flops 115330 | bytes 67164 | solution.py:61
  (735 shorter events, 203.0 us)
Async XLA Ops:
  0.0 31.8 %copy-start = (f32[64,4,4,128]{3,2,1,0:T(4,128)S(1)}, f32[64,4,4,128]{3,2,1,0:T(4,128)}, u32[]{:S(2)}) copy-start(f32[64,4,4,128]{3,2,1,0:T(4,128)} %param.12) | copy-start | bytes 1572868
  0.0 24.9 %copy-start.7 = (f32[64,4,128]{2,1,0:T(4,128)S(1)}, f32[64,4,128]{2,1,0:T(4,128)}, u32[]{:S(2)}) copy-start(f32[64,4,128]{2,1,0:T(4,128)} %param.13) | copy-start | bytes 393220
  10.1 14.9 %collective-permute-start = (f32[4,1,128]{2,1,0:T(1,128)S(1)}, f32[4,1,128]{2,1,0:T(1,128)S(1)}, u32[]{:S(2)}, u32[]{:S(2)}) collective-permute-start(f32[4,1,128]{2,1,0:T(1,128)S(1)} %get-tuple-element.246), channel_id=1, source_target_pairs={{0,32},{32,64},{64,96},{96,128},{128,160},{160,192},{192,224},{224... | collective-permute-start | bytes 6152 | tf_op jit(solution)/shard_map/ppermute | solution.py:16
  12.0 12.9 %collective-permute-start.1 = (f32[4,1,128]{2,1,0:T(1,128)S(1)}, f32[4,1,128]{2,1,0:T(1,128)S(1)}, u32[]{:S(2)}, u32[]{:S(2)}) collective-permute-start(f32[4,1,128]{2,1,0:T(1,128)S(1)} %get-tuple-element.247), channel_id=1, source_target_pairs={{32,0},{64,32},{96,64},{128,96},{160,128},{192,160},{224,192},{256... | collective-permute-start | bytes 6152 | tf_op jit(solution)/shard_map/ppermute | solution.py:19
  18.1 13.7 %collective-permute-start.4 = (f32[64,4,1,128]{3,0,2,1:T(8,128)S(1)}, f32[64,4,1,128]{3,0,2,1:T(8,128)S(1)}, u32[]{:S(2)}, u32[]{:S(2)}) collective-permute-start(f32[64,4,1,128]{3,0,2,1:T(8,128)S(1)} %get-tuple-element.243), channel_id=1, source_target_pairs={{0,32},{32,64},{64,96},{96,128},{128,160},{160,192},{192,224},{224... | collective-permute-start | bytes 393224 | tf_op jit(solution)/shard_map/ppermute | solution.py:16
  20.0 12.0 %collective-permute-start.5 = (f32[64,4,1,128]{3,0,2,1:T(8,128)S(1)}, f32[64,4,1,128]{3,0,2,1:T(8,128)S(1)}, u32[]{:S(2)}, u32[]{:S(2)}) collective-permute-start(f32[64,4,1,128]{3,0,2,1:T(8,128)S(1)} %get-tuple-element.242), channel_id=1, source_target_pairs={{32,0},{64,32},{96,64},{128,96},{160,128},{192,160},{224,192},{256... | collective-permute-start | bytes 393224 | tf_op jit(solution)/shard_map/ppermute | solution.py:19
  25.6 14.2 %collective-permute-start.2 = (f32[4,6,1]{2,1,0:T(8,128)}, f32[4,6,1]{2,1,0:T(8,128)}, u32[]{:S(2)}, u32[]{:S(2)}) collective-permute-start(f32[4,6,1]{2,1,0:T(8,128)} %get-tuple-element.244), channel_id=1, source_target_pairs={{0,1},{1,2},{2,3},{3,4},{4,5},{5,6},{6,7},{7,8},{8,9},{9,10},{10,1... | collective-permute-start | bytes 296 | tf_op jit(solution)/shard_map/ppermute | solution.py:16
  30.5 9.4 %collective-permute-start.3 = (f32[4,6,1]{2,1,0:T(8,128)}, f32[4,6,1]{2,1,0:T(8,128)}, u32[]{:S(2)}, u32[]{:S(2)}) collective-permute-start(f32[4,6,1]{2,1,0:T(8,128)} %get-tuple-element.245), channel_id=1, source_target_pairs={{1,0},{2,1},{3,2},{4,3},{5,4},{6,5},{7,6},{8,7},{9,8},{10,9},{11,1... | collective-permute-start | bytes 296 | tf_op jit(solution)/shard_map/ppermute | solution.py:19
  33.7 7.0 %collective-permute-start.6 = (f32[64,4,6,1]{0,1,3,2:T(4,128)S(1)}, f32[64,4,6,1]{0,1,3,2:T(4,128)S(1)}, u32[]{:S(2)}, u32[]{:S(2)}) collective-permute-start(f32[64,4,6,1]{0,1,3,2:T(4,128)S(1)} %copy.44), channel_id=1, source_target_pairs={{0,1},{1,2},{2,3},{3,4},{4,5},{5,6},{6,7},{7,8},{8,9},{9,10},{10,1... | collective-permute-start | bytes 18440 | tf_op jit(solution)/shard_map/ppermute | solution.py:16
  38.6 5.7 %collective-permute-start.7 = (f32[64,4,6,1]{0,1,3,2:T(4,128)S(1)}, f32[64,4,6,1]{0,1,3,2:T(4,128)S(1)}, u32[]{:S(2)}, u32[]{:S(2)}) collective-permute-start(f32[64,4,6,1]{0,1,3,2:T(4,128)S(1)} %copy.45), channel_id=1, source_target_pairs={{1,0},{2,1},{3,2},{4,3},{5,4},{6,5},{7,6},{8,7},{9,8},{10,9},{11,1... | collective-permute-start | bytes 18440 | tf_op jit(solution)/shard_map/ppermute | solution.py:19
  40.7 4.6 copy-start.1
  45.4 1.0 copy-start.6
  47.4 7.5 %collective-permute-start.8 = (f32[64,4,1,128]{3,0,2,1:T(8,128)S(1)}, f32[64,4,1,128]{3,0,2,1:T(8,128)S(1)}, u32[]{:S(2)}, u32[]{:S(2)}) collective-permute-start(f32[64,4,1,128]{3,0,2,1:T(8,128)S(1)} %get-tuple-element.240), channel_id=1, source_target_pairs={{0,32},{32,64},{64,96},{96,128},{128,160},{160,192},{192,224},{224... | collective-permute-start | bytes 393224 | tf_op jit(solution)/shard_map/ppermute | solution.py:16
  49.3 7.4 %collective-permute-start.9 = (f32[64,4,1,128]{3,0,2,1:T(8,128)S(1)}, f32[64,4,1,128]{3,0,2,1:T(8,128)S(1)}, u32[]{:S(2)}, u32[]{:S(2)}) collective-permute-start(f32[64,4,1,128]{3,0,2,1:T(8,128)S(1)} %get-tuple-element.241), channel_id=1, source_target_pairs={{32,0},{64,32},{96,64},{128,96},{160,128},{192,160},{224,192},{256... | collective-permute-start | bytes 393224 | tf_op jit(solution)/shard_map/ppermute | solution.py:19
  57.1 7.4 %copy-start.8 = (s32[256]{0:T(256)S(1)}, s32[256]{0:T(256)}, u32[]{:S(2)}) copy-start(s32[256]{0:T(256)} %param.16) | copy-start | bytes 3076
  57.1 13.2 %copy-start.2 = (f32[4,6,130]{2,1,0:T(8,128)S(1)}, f32[4,6,130]{2,1,0:T(8,128)}, u32[]{:S(2)}) copy-start(f32[4,6,130]{2,1,0:T(8,128)} %copy-done.1) | copy-start | bytes 37444
  57.4 7.1 %collective-permute-start.10 = (f32[64,4,6,1]{0,1,3,2:T(4,128)S(1)}, f32[64,4,6,1]{0,1,3,2:T(4,128)S(1)}, u32[]{:S(2)}, u32[]{:S(2)}) collective-permute-start(f32[64,4,6,1]{0,1,3,2:T(4,128)S(1)} %copy.60), channel_id=1, source_target_pairs={{0,1},{1,2},{2,3},{3,4},{4,5},{5,6},{6,7},{7,8},{8,9},{9,10},{10,1... | collective-permute-start | bytes 18440 | tf_op jit(solution)/shard_map/ppermute | solution.py:16
  63.2 6.8 %collective-permute-start.11 = (f32[64,4,6,1]{0,1,3,2:T(4,128)S(1)}, f32[64,4,6,1]{0,1,3,2:T(4,128)S(1)}, u32[]{:S(2)}, u32[]{:S(2)}) collective-permute-start(f32[64,4,6,1]{0,1,3,2:T(4,128)S(1)} %copy.61), channel_id=1, source_target_pairs={{1,0},{2,1},{3,2},{4,3},{5,4},{6,5},{7,6},{8,7},{9,8},{10,9},{11,1... | collective-permute-start | bytes 18440 | tf_op jit(solution)/shard_map/ppermute | solution.py:19
  72.4 7.5 %collective-permute-start.12 = (f32[64,4,1,128]{3,0,2,1:T(8,128)S(1)}, f32[64,4,1,128]{3,0,2,1:T(8,128)S(1)}, u32[]{:S(2)}, u32[]{:S(2)}) collective-permute-start(f32[64,4,1,128]{3,0,2,1:T(8,128)S(1)} %get-tuple-element.238), channel_id=1, source_target_pairs={{0,32},{32,64},{64,96},{96,128},{128,160},{160,192},{192,224},{224... | collective-permute-start | bytes 393224 | tf_op jit(solution)/shard_map/ppermute | solution.py:16
  74.3 7.4 %collective-permute-start.13 = (f32[64,4,1,128]{3,0,2,1:T(8,128)S(1)}, f32[64,4,1,128]{3,0,2,1:T(8,128)S(1)}, u32[]{:S(2)}, u32[]{:S(2)}) collective-permute-start(f32[64,4,1,128]{3,0,2,1:T(8,128)S(1)} %get-tuple-element.239), channel_id=1, source_target_pairs={{32,0},{64,32},{96,64},{128,96},{160,128},{192,160},{224,192},{256... | collective-permute-start | bytes 393224 | tf_op jit(solution)/shard_map/ppermute | solution.py:19
  82.4 7.4 %collective-permute-start.14 = (f32[64,4,6,1]{0,1,3,2:T(4,128)S(1)}, f32[64,4,6,1]{0,1,3,2:T(4,128)S(1)}, u32[]{:S(2)}, u32[]{:S(2)}) collective-permute-start(f32[64,4,6,1]{0,1,3,2:T(4,128)S(1)} %copy.66), channel_id=1, source_target_pairs={{0,1},{1,2},{2,3},{3,4},{4,5},{5,6},{6,7},{7,8},{8,9},{9,10},{10,1... | collective-permute-start | bytes 18440 | tf_op jit(solution)/shard_map/ppermute | solution.py:16
  87.8 5.6 %collective-permute-start.15 = (f32[64,4,6,1]{0,1,3,2:T(4,128)S(1)}, f32[64,4,6,1]{0,1,3,2:T(4,128)S(1)}, u32[]{:S(2)}, u32[]{:S(2)}) collective-permute-start(f32[64,4,6,1]{0,1,3,2:T(4,128)S(1)} %copy.67), channel_id=1, source_target_pairs={{1,0},{2,1},{3,2},{4,3},{5,4},{6,5},{7,6},{8,7},{9,8},{10,9},{11,1... | collective-permute-start | bytes 18440 | tf_op jit(solution)/shard_map/ppermute | solution.py:19
  95.8 1.3 copy-start.9
  95.8 1.3 copy-start.10
  (3 other events, 2.2 us)
